TPU v7x, 128 devices: a whole 4x4x4 slice. The times are simulated.
128 devices in a mesh: section: 2 (over y_lo), dp: 32 (over z, y_hi, x), tensor: 2 (over core).
Axes of the slice: x: 4, y: 4 (y_hi: 2, y_lo: 2; y = y_hi * 2 + y_lo), z: 4, core: 2. Of those that a mesh axis runs over, the one named last changes fastest.
Arguments:
- tokens: bfloat16 [16384, 768], P('dp'), may hold values from -6 to 6
- cotangent: bfloat16 [16384, 768], P('dp'), may hold values from -6 to 6
- segments: int32 [64, 256], P('dp'), may hold values from 0 to 3, never falling along the last dimension, each value on 1 to 128 neighbouring positions
- routes: int32 [2, 16384], P('section', 'dp'), may hold values from 0 to 31, as said below
- keeps: int32 [2, 16384], P('section', 'dp'), may hold values from 0 to 1, as said below
- attn_gain: bfloat16 [2, 768], P('section', 'dp'), may hold values from 0.25 to 1.75
- moe_gain: bfloat16 [2, 768], P('section', 'dp'), may hold values from 0.25 to 1.75
- qkv_weight: bfloat16 [2, 3, 768, 768], P('section', None, 'dp', 'tensor'), may hold values from -0.3125 to 0.3125
- out_weight: bfloat16 [2, 768, 768], P('section', 'tensor', 'dp'), may hold values from -0.875 to 0.875
- router_weight: bfloat16 [2, 768, 32], P('section', 'dp'), may hold values from -0.109375 to 0.109375
- expert_in: bfloat16 [2, 32, 768, 3072], P('section', 'dp', None, 'tensor'), may hold values from -0.21875 to 0.21875
- expert_out: bfloat16 [2, 32, 3072, 768], P('section', 'dp', 'tensor'), may hold values from -4.156922 to 4.156922, as said below
Outputs:
- layer_outputs: float32 [2, 16384, 768], P('section', 'dp', 'tensor')
- input_grads: float32 [2, 16384, 768], P('section', 'dp', 'tensor')
- attn_gain_grad: float32 [2, 768], P('section', 'dp')
- moe_gain_grad: float32 [2, 768], P('section', 'dp')
- qkv_grad: float32 [2, 3, 768, 768], P('section', None, 'dp', 'tensor')
- out_grad: float32 [2, 768, 768], P('section', 'tensor', 'dp')
- router_grad: float32 [2, 768, 32], P('section', 'dp')
- expert_in_grad: float32 [2, 32, 768, 3072], P('section', 'dp', None, 'tensor')
- expert_out_grad: float32 [2, 32, 3072, 768], P('section', 'dp', 'tensor')
Inputs may be any that keep to these rules, and one draw needn't show every extreme that they name: `routes`: in each layer one expert is named by 10 or more tokens of every sequence. keeps[l, i] is 1 exactly when fewer than 10 earlier tokens of the same sequence name the same expert in layer l; so at most 10 kept tokens of one sequence go to one expert. `expert_out`: independent entries of mean zero.
All inputs are finite; a program needn't handle non-finite values.
Results may differ from a plain program's by a relative error of at most 0.035.
Values may be sent and summed in bfloat16 or wider, within the bound.
No kernel may reach another device: no remote copies, remote signals or barrier semaphores. Data moves between devices by JAX's collectives and lax.ppermute only.
A program may use at most 192 MiB of HBM per device.

v0:
```python
import jax
import jax.numpy as jnp
from jax import lax
from jax.sharding import PartitionSpec as P

HEAD_DIM = 64


EPS = 1e-06
MASK_FILL = -1e30


def partner(value, axis, stride):
    mask = 2**stride
    pairs = [(source, source ^ mask) for source in range(lax.axis_size(axis))]
    return lax.ppermute(value, axis, pairs)


def rms_parts(rows_in, gain_row):
    inv_scale = lax.rsqrt(jnp.mean(rows_in * rows_in, axis=-1, keepdims=True) + EPS)
    normed = rows_in * inv_scale
    return (inv_scale, normed, normed * gain_row)


def rms_back(grad_out, inv_scale, normed, gain_row):
    grad_normed = grad_out * gain_row
    gain_grad = jnp.sum(grad_out * normed, axis=0)
    grad_in = inv_scale * (
        grad_normed - normed * jnp.mean(grad_normed * normed, axis=-1, keepdims=True)
    )
    return (grad_in, gain_grad)


def gelu_tanh(values):
    return jax.nn.gelu(values, approximate=True)


def build_slots(route_row, keep_row, experts, capacity):
    chosen = (route_row[:, None] == jnp.arange(experts, dtype=jnp.int32)[None, :]).astype(jnp.int32)
    kept_hot = chosen * keep_row[:, None]
    before = jnp.cumsum(kept_hot, axis=0) - kept_hot
    rank_row = jnp.sum(before * kept_hot, axis=1)
    slot_row = route_row * capacity + rank_row
    placed = (slot_row[:, None] == jnp.arange(experts * capacity, dtype=jnp.int32)[None, :]) & (
        keep_row[:, None] == 1
    )
    return (chosen.astype(jnp.float32), placed.astype(jnp.bfloat16))


def head_scores(queries, key_rows, seg_row):
    scores = jnp.einsum(
        "qhe,khe->hqk", queries, key_rows, preferred_element_type=jnp.float32
    ) * HEAD_DIM ** (-0.5)
    same_doc = (seg_row[:, None] == seg_row[None, :])[None]
    return (scores, same_doc)


def to_other_section(rows_in):
    return partner(rows_in, "section", 0)


def layer_forward(hidden_in, seg_row, route_row, keep_row, dense_full, expert_in, expert_out):
    attn_gain, moe_gain, qkv_full, out_full, router_full = dense_full
    row_count, model_width = hidden_in.shape
    local_width = qkv_full.shape[2]
    head_count = local_width // HEAD_DIM
    experts = router_full.shape[1]
    capacity = max(2, 5 * row_count // (4 * experts))
    scale_one, normed_one, pre_one = rms_parts(hidden_in, attn_gain.astype(jnp.float32))
    normed_low = pre_one.astype(jnp.bfloat16)
    qkv_rows = jnp.einsum(
        "sd,cde->cse", normed_low, qkv_full, preferred_element_type=jnp.float32
    ).astype(jnp.bfloat16)
    queries = qkv_rows[0].reshape(row_count, head_count, HEAD_DIM)
    key_rows = qkv_rows[1].reshape(row_count, head_count, HEAD_DIM)
    value_rows = qkv_rows[2].reshape(row_count, head_count, HEAD_DIM)
    scores, same_doc = head_scores(queries, key_rows, seg_row)
    masked = jnp.where(same_doc, scores, MASK_FILL)
    row_max = jnp.max(masked, axis=-1, keepdims=True)
    exponent = jnp.exp(masked - row_max)
    row_total = jnp.sum(exponent, axis=-1, keepdims=True)
    soft_rows = (exponent / row_total).astype(jnp.bfloat16)
    log_total = row_max + jnp.log(row_total)
    mixed_heads = (
        jnp.einsum("hqk,khe->qhe", soft_rows, value_rows, preferred_element_type=jnp.float32)
        .astype(jnp.bfloat16)
        .reshape(row_count, local_width)
    )
    partial_attn = jnp.dot(mixed_heads, out_full, preferred_element_type=jnp.float32)
    attention = lax.psum(partial_attn, "tensor")
    hidden = hidden_in + attention
    scale_two, normed_two, pre_two = rms_parts(hidden, moe_gain.astype(jnp.float32))
    moe_in = pre_two.astype(jnp.bfloat16)
    logits = jnp.dot(moe_in, router_full, preferred_element_type=jnp.float32)
    router_prob = jax.nn.softmax(logits, axis=-1)
    chosen, placed = build_slots(route_row, keep_row, experts, capacity)
    gate_prob = jnp.sum(router_prob * chosen, axis=1)
    sending = (
        jnp.einsum("sc,sd->cd", placed, moe_in, preferred_element_type=jnp.float32)
        .astype(jnp.bfloat16)
        .reshape(experts, capacity, model_width)
    )
    arrived = lax.all_to_all(sending, "dp", split_axis=0, concat_axis=1, tiled=True)
    expert_hidden = jnp.einsum(
        "erd,edf->erf", arrived, expert_in, preferred_element_type=jnp.float32
    )
    activated = gelu_tanh(expert_hidden).astype(jnp.bfloat16)
    partial_rows = jnp.einsum(
        "erf,efd->erd", activated, expert_out, preferred_element_type=jnp.float32
    )
    summed_rows = lax.psum(partial_rows, "tensor").astype(jnp.bfloat16)
    returned_rows = lax.all_to_all(summed_rows, "dp", split_axis=1, concat_axis=0, tiled=True)
    returned = jnp.einsum(
        "sc,cd->sd",
        placed,
        returned_rows.reshape(experts * capacity, model_width),
        preferred_element_type=jnp.float32,
    )
    layer_out = hidden + gate_prob[:, None] * returned
    saved_state = (
        normed_low,
        scale_one,
        normed_one,
        queries,
        key_rows,
        value_rows,
        log_total,
        mixed_heads,
        scale_two,
        normed_two,
        moe_in,
        router_prob,
        chosen,
        gate_prob,
        placed,
        arrived,
        expert_hidden,
        activated,
        returned,
    )
    return (layer_out, saved_state)


def layer_backward(grad_out, saved_state, seg_row, dense_full, expert_in, expert_out):
    (
        normed_low,
        scale_one,
        normed_one,
        queries,
        key_rows,
        value_rows,
        log_total,
        mixed_heads,
        scale_two,
        normed_two,
        moe_in,
        router_prob,
        chosen,
        gate_prob,
        placed,
        arrived,
        expert_hidden,
        activated,
        returned,
    ) = saved_state
    attn_gain, moe_gain, qkv_full, out_full, router_full = dense_full
    row_count, model_width = grad_out.shape
    local_width = qkv_full.shape[2]
    head_count = local_width // HEAD_DIM
    experts = router_full.shape[1]
    capacity = placed.shape[1] // experts
    scaling = HEAD_DIM ** (-0.5)
    grad_tokens = (gate_prob[:, None] * grad_out).astype(jnp.bfloat16)
    grad_gate = jnp.sum(grad_out * returned, axis=1)
    grad_sending = (
        jnp.einsum("sc,sd->cd", placed, grad_tokens, preferred_element_type=jnp.float32)
        .astype(jnp.bfloat16)
        .reshape(experts, capacity, model_width)
    )
    grad_arrived = lax.all_to_all(grad_sending, "dp", split_axis=0, concat_axis=1, tiled=True)
    grad_activated = jnp.einsum(
        "erd,efd->erf", grad_arrived, expert_out, preferred_element_type=jnp.float32
    )
    expert_out_grad = jnp.einsum(
        "erf,erd->efd", activated, grad_arrived, preferred_element_type=jnp.float32
    )
    gelu_pull = jax.vjp(gelu_tanh, expert_hidden)[1]
    grad_pre = gelu_pull(grad_activated)[0].astype(jnp.bfloat16)
    expert_in_grad = jnp.einsum(
        "erd,erf->edf", arrived, grad_pre, preferred_element_type=jnp.float32
    )
    partial_grad = jnp.einsum(
        "erf,edf->erd", grad_pre, expert_in, preferred_element_type=jnp.float32
    )
    grad_rows = lax.psum(partial_grad, "tensor").astype(jnp.bfloat16)
    grad_back = lax.all_to_all(grad_rows, "dp", split_axis=1, concat_axis=0, tiled=True)
    grad_moe_in = jnp.einsum(
        "sc,cd->sd",
        placed,
        grad_back.reshape(experts * capacity, model_width),
        preferred_element_type=jnp.float32,
    )
    grad_logits = ((grad_gate * gate_prob)[:, None] * (chosen - router_prob)).astype(jnp.bfloat16)
    router_grad = jnp.einsum("sd,se->de", moe_in, grad_logits, preferred_element_type=jnp.float32)
    grad_moe_in = grad_moe_in + jnp.einsum(
        "se,de->sd", grad_logits, router_full, preferred_element_type=jnp.float32
    )
    grad_norm_two, moe_gain_grad = rms_back(
        grad_moe_in, scale_two, normed_two, moe_gain.astype(jnp.float32)
    )
    grad_hidden = grad_out + grad_norm_two
    grad_attention = grad_hidden.astype(jnp.bfloat16)
    out_grad = jnp.einsum(
        "sk,sd->kd", mixed_heads, grad_attention, preferred_element_type=jnp.float32
    )
    grad_mixed = (
        jnp.einsum("sd,kd->sk", grad_attention, out_full, preferred_element_type=jnp.float32)
        .astype(jnp.bfloat16)
        .reshape(row_count, head_count, HEAD_DIM)
    )
    scores, same_doc = head_scores(queries, key_rows, seg_row)
    soft_rows = jnp.where(same_doc, jnp.exp(scores - log_total), 0.0)
    grad_soft = jnp.einsum(
        "qhe,khe->hqk", grad_mixed, value_rows, preferred_element_type=jnp.float32
    )
    row_delta = jnp.sum(soft_rows * grad_soft, axis=-1, keepdims=True)
    grad_scores = (soft_rows * (grad_soft - row_delta)).astype(jnp.bfloat16)
    grad_values = jnp.einsum(
        "hqk,qhe->khe",
        soft_rows.astype(jnp.bfloat16),
        grad_mixed,
        preferred_element_type=jnp.float32,
    )
    grad_queries = (
        jnp.einsum("hqk,khe->qhe", grad_scores, key_rows, preferred_element_type=jnp.float32)
        * scaling
    )
    grad_keys = (
        jnp.einsum("hqk,qhe->khe", grad_scores, queries, preferred_element_type=jnp.float32)
        * scaling
    )
    grad_qkv = (
        jnp.stack([grad_queries, grad_keys, grad_values])
        .astype(jnp.bfloat16)
        .reshape(3, row_count, local_width)
    )
    qkv_grad = jnp.einsum("sd,cse->cde", normed_low, grad_qkv, preferred_element_type=jnp.float32)
    partial_norm = jnp.einsum("cse,cde->sd", grad_qkv, qkv_full, preferred_element_type=jnp.float32)
    grad_normed = lax.psum(partial_norm, "tensor")
    grad_norm_one, attn_gain_grad = rms_back(
        grad_normed, scale_one, normed_one, attn_gain.astype(jnp.float32)
    )
    grad_in = grad_hidden + grad_norm_one
    return (
        grad_in,
        (
            attn_gain_grad,
            moe_gain_grad,
            qkv_grad,
            out_grad,
            router_grad,
            expert_in_grad,
            expert_out_grad,
        ),
    )


def pick_tick(first_section, items, first_at, second_at):
    last_index = len(items) - 1
    early_pick = items[min(max(first_at, 0), last_index)]
    later_pick = items[min(max(second_at, 0), last_index)]
    return jax.tree.map(
        lambda early_item, later_item: jnp.where(first_section, early_item, later_item),
        early_pick,
        later_pick,
    )


def local(
    tokens,
    cotangent,
    segments,
    routes,
    keeps,
    attn_gain,
    moe_gain,
    qkv_weight,
    out_weight,
    router_weight,
    expert_in,
    expert_out,
):
    first_section = lax.axis_index("section") == 0
    micro_count, seq_len = segments.shape
    model_width = tokens.shape[1]
    dense_full = (
        lax.all_gather(attn_gain[0], "dp", axis=0, tiled=True),
        lax.all_gather(moe_gain[0], "dp", axis=0, tiled=True),
        lax.all_gather(qkv_weight[0], "dp", axis=1, tiled=True),
        lax.all_gather(out_weight[0], "dp", axis=1, tiled=True),
        lax.all_gather(router_weight[0], "dp", axis=0, tiled=True),
    )
    local_in = expert_in[0]
    local_out = expert_out[0]
    inputs = tokens.astype(jnp.float32).reshape(micro_count, seq_len, model_width)
    targets = cotangent.astype(jnp.float32).reshape(micro_count, seq_len, model_width)
    route_rows = routes[0].reshape(micro_count, seq_len)
    keep_rows = keeps[0].reshape(micro_count, seq_len)
    row_sets = [
        (segments[micro_index], route_rows[micro_index], keep_rows[micro_index])
        for micro_index in range(micro_count)
    ]
    received = jnp.zeros((seq_len, model_width), jnp.float32)
    forward_out = []
    forward_kept = []
    for moment in range(micro_count + 1):
        seg_row, route_row, keep_row = pick_tick(first_section, row_sets, moment, moment - 1)
        layer_in = jnp.where(first_section, inputs[min(moment, micro_count - 1)], received)
        layer_out, saved_state = layer_forward(
            layer_in, seg_row, route_row, keep_row, dense_full, local_in, local_out
        )
        forward_out.append(layer_out)
        forward_kept.append((saved_state, seg_row))
        if moment < micro_count:
            received = to_other_section(layer_out)
    coming = jnp.zeros((seq_len, model_width), jnp.float32)
    grad_sum = None
    backward_in = []
    for moment in range(micro_count + 1):
        is_valid = jnp.where(first_section, moment >= 1, moment < micro_count).astype(jnp.float32)
        grad_out = (
            jnp.where(first_section, coming, targets[min(moment, micro_count - 1)]) * is_valid
        )
        saved_state, seg_row = pick_tick(first_section, forward_kept, moment - 1, moment + 1)
        grad_in, layer_grads = layer_backward(
            grad_out, saved_state, seg_row, dense_full, local_in, local_out
        )
        grad_sum = layer_grads if grad_sum is None else jax.tree.map(jnp.add, grad_sum, layer_grads)
        backward_in.append(grad_in)
        if moment < micro_count:
            coming = to_other_section(grad_in)
    tensor_half = model_width // lax.axis_size("tensor")
    offset = lax.axis_index("tensor") * tensor_half
    out_rows = [
        jnp.where(first_section, forward_out[micro_index], forward_out[micro_index + 1])
        for micro_index in range(micro_count)
    ]
    grad_rows = [
        jnp.where(first_section, backward_in[micro_index + 1], backward_in[micro_index])
        for micro_index in range(micro_count)
    ]
    layer_outputs = lax.dynamic_slice_in_dim(
        jnp.concatenate(out_rows, axis=0), offset, tensor_half, 1
    )[None]
    input_grads = lax.dynamic_slice_in_dim(
        jnp.concatenate(grad_rows, axis=0), offset, tensor_half, 1
    )[None]
    (
        attn_gain_grad,
        moe_gain_grad,
        qkv_grad,
        out_grad,
        router_grad,
        expert_in_grad,
        expert_out_grad,
    ) = grad_sum
    owned_grads = (
        lax.psum_scatter(
            attn_gain_grad.astype(jnp.bfloat16), "dp", scatter_dimension=0, tiled=True
        ).astype(jnp.float32),
        lax.psum_scatter(
            moe_gain_grad.astype(jnp.bfloat16), "dp", scatter_dimension=0, tiled=True
        ).astype(jnp.float32),
        lax.psum_scatter(
            qkv_grad.astype(jnp.bfloat16), "dp", scatter_dimension=1, tiled=True
        ).astype(jnp.float32),
        lax.psum_scatter(
            out_grad.astype(jnp.bfloat16), "dp", scatter_dimension=1, tiled=True
        ).astype(jnp.float32),
        lax.psum_scatter(
            router_grad.astype(jnp.bfloat16), "dp", scatter_dimension=0, tiled=True
        ).astype(jnp.float32),
    )
    return (
        layer_outputs,
        input_grads,
        owned_grads[0][None],
        owned_grads[1][None],
        owned_grads[2][None],
        owned_grads[3][None],
        owned_grads[4][None],
        expert_in_grad[None],
        expert_out_grad[None],
    )


def solution(mesh):
    placed = (
        P("dp", None),
        P("dp", None),
        P("dp", None),
        P("section", "dp"),
        P("section", "dp"),
        P("section", "dp"),
        P("section", "dp"),
        P("section", None, "dp", "tensor"),
        P("section", "tensor", "dp"),
        P("section", "dp", None),
        P("section", "dp", None, "tensor"),
        P("section", "dp", "tensor", None),
    )
    return jax.shard_map(
        local,
        mesh=mesh,
        in_specs=placed,
        out_specs=(
            P("section", "dp", "tensor"),
            P("section", "dp", "tensor"),
            P("section", "dp"),
            P("section", "dp"),
            P("section", None, "dp", "tensor"),
            P("section", "tensor", "dp"),
            P("section", "dp", None),
            P("section", "dp", None, "tensor"),
            P("section", "dp", "tensor", None),
        ),
        check_vma=False,
    )
```

profile of v0, /device:TPU:0, one launch (start us, length us, event | category | flops | bytes accessed | tf_op | source)
XLA Modules:
  0.0 1725.6 jit_solution(6637987960484740011)
XLA Ops:
  11.7 98.0 %all-reduce.11 = (bf16[768]{0:T(1024)(128)(2,1)S(1)}, bf16[768]{0:T(1024)(128)(2,1)S(1)}) all-reduce(bf16[768]{0:T(1024)(128)(2,1)S(1)} %dynamic-update-slice, bf16[768]{0:T(1024)(128)(2,1)S(1)} %dynamic-update-slice.1), channel_id=2, replica_groups=mesh['section'=2,'dp'=32,'tensor'=2] {'dp'}, use_global_device_ids=true, to_apply=%add | all-reduce | flops 1536 | bytes 6144
  118.6 90.4 %all-gather.2 = bf16[1,384,768]{1,2,0:T(8,128)(2,1)S(1)} all-gather(bf16[1,384,24]{1,2,0:T(8,128)(2,1)S(1)} %copy-done.124), channel_id=4, replica_groups=mesh['section'=2,'dp'=32,'tensor'=2] {'dp'}, dimensions={2}, use_global_device_ids=true | all-gather | bytes 608256 | tf_op jit(solution)/shard_map/all_gather | solution.py:300
  221.8 18.1 %all-reduce.23.cloned.1.call-done = f32[256,768]{1,0:T(8,128)} async-done(((f32[256,768]{1,0:T(8,128)}), f32[256,768]{1,0:T(8,128)}) %all-reduce.23.cloned.1.call-update) | async-done | bytes 786448 | tf_op jit(solution)/shard_map/psum | solution.py:90
  245.7 25.6 %all_to_all.48 = bf16[32,10,768]{2,1,0:T(8,128)(2,1)} all-to-all(bf16[32,10,768]{2,1,0:T(8,128)(2,1)} %reshape.964), channel_id=1, replica_groups=mesh['section'=2,'dp'=32,'tensor'=2] {'dp'}, dimensions={0} | all-to-all | bytes 983040 | tf_op jit(solution)/shard_map/all_to_all | solution.py:103
  279.5 7.3 all-reduce.34
  290.1 5.3 reduce.6
  297.4 5.3 all-to-all-start.1
  302.8 96.3 %all-gather.4 = bf16[1,768,32]{2,1,0:T(8,128)(2,1)S(1)} all-gather(bf16[1,24,32]{2,1,0:T(8,128)(2,1)} %param.21), channel_id=6, replica_groups=mesh['section'=2,'dp'=32,'tensor'=2] {'dp'}, dimensions={1}, use_global_device_ids=true | all-gather | bytes 50688 | tf_op jit(solution)/shard_map/all_gather | solution.py:301
  410.9 8.4 collective-permute-done
  443.7 6.4 all-reduce.25.cloned.1.call-done
  458.2 9.9 all-to-all-start.2
  476.5 7.2 all-to-all-done.2
  483.8 5.1 all-to-all-start.6
  497.2 6.7 all-to-all-done.6
  512.6 10.0 all-reduce.35
  525.3 5.3 reduce.7
  532.6 4.6 all-to-all-start.3
  541.5 5.3 reduce.8
  550.6 8.1 all-to-all-start.7
  575.1 5.0 multiply_reduce_fusion.5
  587.3 10.7 collective-permute-done.1
  628.0 6.6 fusion.147
  634.5 17.3 all-reduce.33.cloned.1.call-done
  663.4 9.5 all-to-all-start.4
  677.0 13.4 all-to-all-done.4
  698.8 6.4 all-to-all-start.8
  711.5 8.8 all-to-all-done.8
  729.0 9.6 all-reduce.36
  741.3 5.3 reduce.9
  748.6 5.0 all-to-all-start.5
  760.1 5.3 reduce.10
  767.5 10.0 all-to-all-start.9
  828.5 5.0 fusion.321
  833.5 4.8 all-reduce.27.cloned.1.call-done
  853.3 10.0 collective-permute-done.3
  868.0 9.5 all-to-all-start.10
  883.4 9.6 all-to-all-done.10
  901.7 7.3 all-reduce.37
  911.7 5.4 reduce.11
  919.1 4.7 all-to-all-start.11
  928.1 9.0 all-to-all-done.11
  960.1 159.5 %reduce-scatter.9.cloned.1.call-done = bf16[24,32]{1,0:T(8,128)(2,1)} async-done(((bf16[768,32]{1,0:T(8,128)(2,1)}), bf16[24,32]{1,0:T(8,128)(2,1)}) %reduce-scatter.9.cloned.1.call-update) | async-done | bytes 1552
  1123.9 9.6 add_bitcast_fusion
  1133.6 7.6 add_bitcast_fusion.1
  1143.2 5.2 copy.214
  1153.9 91.8 %all-reduce.10 = (bf16[768]{0:T(1024)(128)(2,1)S(1)}, bf16[768]{0:T(1024)(128)(2,1)S(1)}) all-reduce(bf16[768]{0:T(1024)(128)(2,1)S(1)} %add_convert_fusion.2, bf16[768]{0:T(1024)(128)(2,1)S(1)} %add_convert_fusion.1), channel_id=7, replica_groups=mesh['section'=2,'dp'=32,'tensor'=2] {'dp'}, use_global_device_ids=true, to_apply=%region_57.58.clone | all-reduce | flops 1536 | bytes 6144
  1249.8 109.3 %reduce-scatter.7.cloned.1.call-done = bf16[384,24]{0,1:T(8,128)(2,1)} async-done(((bf16[384,768]{0,1:T(8,128)(2,1)}), bf16[384,24]{0,1:T(8,128)(2,1)}) %reduce-scatter.7.cloned.1.call-update) | async-done | bytes 18448
  1360.4 356.6 %all-reduce.31.cloned.1.call-done = bf16[3,768,384]{2,0,1:T(4,128)(2,1)} async-done(((bf16[3,768,384]{2,0,1:T(4,128)(2,1)}), bf16[3,768,384]{2,0,1:T(4,128)(2,1)}) %all-reduce.31.cloned.1.call-update) | async-done | bytes 1769488
  (627 shorter events, 366.9 us)
Async XLA Ops:
  7.2 270.1 %copy-start = (bf16[1,1,1536,768]{3,2,1,0:T(8,128)(2,1)S(1)}, bf16[1,1,1536,768]{3,2,1,0:T(8,128)(2,1)}, u32[]{:S(2)}) copy-start(bf16[1,1,1536,768]{3,2,1,0:T(8,128)(2,1)} %param.23) | copy-start | bytes 7077892
  7.2 105.0 %copy-start.173 = (s32[1,512]{1,0:T(1,128)S(1)}, s32[1,512]{1,0:T(1,128)}, u32[]{:S(2)}) copy-start(s32[1,512]{1,0:T(1,128)} %param.15) | copy-start | bytes 6148
  7.2 105.0 %copy-start.174 = (s32[1,512]{1,0:T(1,128)S(1)}, s32[1,512]{1,0:T(1,128)}, u32[]{:S(2)}) copy-start(s32[1,512]{1,0:T(1,128)} %param.16) | copy-start | bytes 6148
  7.2 108.1 %copy-start.172 = (s32[2,256]{1,0:T(2,128)S(1)}, s32[2,256]{1,0:T(2,128)}, u32[]{:S(2)}) copy-start(s32[2,256]{1,0:T(2,128)} %param.14) | copy-start | bytes 6148
  7.2 201.8 %all-gather.7.cloned.1.call-start = ((), (), s32[]{:S(2)}) async-start(), calls=%async_computation.18 | async-start | bytes 1824768 | tf_op jit(solution)/shard_map/all_gather | solution.py:299
  8.0 231.9 %all-reduce.23.cloned.1.call-start = ((), (), s32[]{:S(2)}) async-start(), calls=%async_computation.14 | async-start | bytes 1572864 | tf_op jit(solution)/shard_map/psum | solution.py:90
  118.5 93.4 %copy-start.47 = (bf16[256,768]{1,0:T(8,128)(2,1)}, bf16[256,768]{1,0:T(8,128)(2,1)S(1)}, u32[]{:S(2)}) copy-start(bf16[256,768]{1,0:T(8,128)(2,1)S(1)} %multiply_convert_fusion.11) | copy-start | bytes 1179652
  221.2 22.4 %copy-start.155 = (pred[256]{0:T(512)(128)(4,1)}, pred[256]{0:T(512)(128)(4,1)S(1)}, u32[]{:S(2)}) copy-start(pred[256]{0:T(512)(128)(4,1)S(1)} %get-tuple-element.133) | copy-start | bytes 772
  221.8 21.9 %copy-start.123 = (s32[256]{0:T(256)}, s32[256]{0:T(256)S(1)}, u32[]{:S(2)}) copy-start(s32[256]{0:T(256)S(1)} %get-tuple-element.136) | copy-start | bytes 3076
  241.4 29.8 %copy-start.133 = (f32[256]{0:T(256)}, f32[256]{0:T(256)S(1)}, u32[]{:S(2)}) copy-start(f32[256]{0:T(256)S(1)} %get-tuple-element.91) | copy-start | bytes 3076
  241.4 29.8 %copy-start.148 = (f32[256]{0:T(256)}, f32[256]{0:T(256)S(1)}, u32[]{:S(2)}) copy-start(f32[256]{0:T(256)S(1)} %add_rsqrt_fusion.4) | copy-start | bytes 3076
  297.4 103.6 %all-to-all-start.1 = ((bf16[32,2,3840]{2,1,0:T(2,128)(2,1)}), bf16[32,2,3840]{2,1,0:T(2,128)(2,1)}, u32[]{:S(2)}, u32[]{:S(2)}) async-start(bf16[32,2,3840]{2,1,0:T(2,128)(2,1)} %reshape.1034), calls=%async_computation.1 | async-start | bytes 983040 | tf_op jit(solution)/shard_map/all_to_all | solution.py:112
  302.7 147.4 %all-reduce.25.cloned.1.call-start = ((), (), s32[]{:S(2)}) async-start(), calls=%async_computation.15 | async-start | bytes 1572864 | tf_op jit(solution)/shard_map/psum | solution.py:90
  404.4 14.9 copy-start.1
  407.3 12.0 collective-permute-start
  458.2 25.6 %all-to-all-start.2 = ((bf16[32,10,768]{2,1,0:T(8,128)(2,1)}), bf16[32,10,768]{2,1,0:T(8,128)(2,1)}, u32[]{:S(2)}, u32[]{:S(2)}) async-start(bf16[32,10,768]{2,1,0:T(8,128)(2,1)} %reshape.971), calls=%async_computation.2 | async-start | bytes 1572864 | tf_op jit(solution)/shard_map/all_to_all | solution.py:103
  483.8 20.1 %all-to-all-start.6 = ((bf16[32,10,768]{2,1,0:T(8,128)(2,1)}), bf16[32,10,768]{2,1,0:T(8,128)(2,1)}, u32[]{:S(2)}, u32[]{:S(2)}) async-start(bf16[32,10,768]{2,1,0:T(8,128)(2,1)} %reshape.979), calls=%async_computation.6 | async-start | bytes 1572864 | tf_op jit(solution)/shard_map/all_to_all | solution.py:180
  532.6 18.0 %all-to-all-start.3 = ((bf16[32,2,3840]{2,1,0:T(2,128)(2,1)}), bf16[32,2,3840]{2,1,0:T(2,128)(2,1)}, u32[]{:S(2)}, u32[]{:S(2)}) async-start(bf16[32,2,3840]{2,1,0:T(2,128)(2,1)} %reshape.1036), calls=%async_computation.3 | async-start | bytes 983040 | tf_op jit(solution)/shard_map/all_to_all | solution.py:112
  550.6 21.1 %all-to-all-start.7 = ((bf16[32,2,3840]{2,1,0:T(2,128)(2,1)}), bf16[32,2,3840]{2,1,0:T(2,128)(2,1)}, u32[]{:S(2)}, u32[]{:S(2)}) async-start(bf16[32,2,3840]{2,1,0:T(2,128)(2,1)} %reshape.1040), calls=%async_computation.7 | async-start | bytes 983040 | tf_op jit(solution)/shard_map/all_to_all | solution.py:196
  558.7 93.1 %all-reduce.33.cloned.1.call-start = ((), (), s32[]{:S(2)}) async-start(), calls=%async_computation.22 | async-start | bytes 3145728 | tf_op jit(solution)/shard_map/psum | solution.py:90
  580.1 17.8 %collective-permute-start.1 = (f32[256,768]{1,0:T(8,128)}, f32[256,768]{1,0:T(8,128)}, u32[]{:S(2)}, u32[]{:S(2)}) collective-permute-start(f32[256,768]{1,0:T(8,128)} %get-tuple-element.98), channel_id=1, source_target_pairs={{0,64},{64,0},{1,65},{65,1},{2,66},{66,2},{3,67},{67,3},{4,68},{68... | collective-permute-start | bytes 2359304 | tf_op jit(solution)/shard_map/ppermute | solution.py:16
  584.6 13.6 copy-start.161
  657.6 34.8 %collective-permute-start.2 = (f32[256,768]{1,0:T(8,128)}, f32[256,768]{1,0:T(8,128)}, u32[]{:S(2)}, u32[]{:S(2)}) collective-permute-start(f32[256,768]{1,0:T(8,128)} %multiply_add_fusion.3), channel_id=1, source_target_pairs={{0,64},{64,0},{1,65},{65,1},{2,66},{66,2},{3,67},{67,3},{4,68},{68... | collective-permute-start | bytes 2359304 | tf_op jit(solution)/shard_map/ppermute | solution.py:16
  663.4 27.0 %all-to-all-start.4 = ((bf16[32,10,768]{2,1,0:T(8,128)(2,1)}), bf16[32,10,768]{2,1,0:T(8,128)(2,1)}, u32[]{:S(2)}, u32[]{:S(2)}) async-start(bf16[32,10,768]{2,1,0:T(8,128)(2,1)} %reshape.976), calls=%async_computation.4 | async-start | bytes 1572864 | tf_op jit(solution)/shard_map/all_to_all | solution.py:103
  698.8 21.5 %all-to-all-start.8 = ((bf16[32,10,768]{2,1,0:T(8,128)(2,1)}), bf16[32,10,768]{2,1,0:T(8,128)(2,1)}, u32[]{:S(2)}, u32[]{:S(2)}) async-start(bf16[32,10,768]{2,1,0:T(8,128)(2,1)} %reshape.983), calls=%async_computation.8 | async-start | bytes 1572864 | tf_op jit(solution)/shard_map/all_to_all | solution.py:180
  748.6 18.9 %all-to-all-start.5 = ((bf16[32,2,3840]{2,1,0:T(2,128)(2,1)}), bf16[32,2,3840]{2,1,0:T(2,128)(2,1)}, u32[]{:S(2)}, u32[]{:S(2)}) async-start(bf16[32,2,3840]{2,1,0:T(2,128)(2,1)} %reshape.1038), calls=%async_computation.5 | async-start | bytes 983040 | tf_op jit(solution)/shard_map/all_to_all | solution.py:112
  767.5 23.0 %all-to-all-start.9 = ((bf16[32,2,3840]{2,1,0:T(2,128)(2,1)}), bf16[32,2,3840]{2,1,0:T(2,128)(2,1)}, u32[]{:S(2)}, u32[]{:S(2)}) async-start(bf16[32,2,3840]{2,1,0:T(2,128)(2,1)} %reshape.1042), calls=%async_computation.9 | async-start | bytes 983040 | tf_op jit(solution)/shard_map/all_to_all | solution.py:196
  777.5 60.7 %all-reduce.27.cloned.1.call-start = ((), (), s32[]{:S(2)}) async-start(), calls=%async_computation.16 | async-start | bytes 1572864 | tf_op jit(solution)/shard_map/psum | solution.py:249
  842.3 21.1 %collective-permute-start.3 = (f32[256,768]{1,0:T(8,128)S(1)}, f32[256,768]{1,0:T(8,128)S(1)}, u32[]{:S(2)}, u32[]{:S(2)}) collective-permute-start(f32[256,768]{1,0:T(8,128)S(1)} %get-tuple-element.74), channel_id=1, source_target_pairs={{0,64},{64,0},{1,65},{65,1},{2,66},{66,2},{3,67},{67,3},{4,68},{68... | collective-permute-start | bytes 2359304 | tf_op jit(solution)/shard_map/ppermute | solution.py:16
  848.9 14.4 copy-start.11
  848.9 14.4 copy-start.38
  848.9 14.4 copy-start.41
  868.0 25.1 %all-to-all-start.10 = ((bf16[32,10,768]{2,1,0:T(8,128)(2,1)}), bf16[32,10,768]{2,1,0:T(8,128)(2,1)}, u32[]{:S(2)}, u32[]{:S(2)}) async-start(bf16[32,10,768]{2,1,0:T(8,128)(2,1)} %reshape.987), calls=%async_computation.10 | async-start | bytes 1572864 | tf_op jit(solution)/shard_map/all_to_all | solution.py:180
  919.1 18.1 %all-to-all-start.11 = ((bf16[32,2,3840]{2,1,0:T(2,128)(2,1)}), bf16[32,2,3840]{2,1,0:T(2,128)(2,1)}, u32[]{:S(2)}, u32[]{:S(2)}) async-start(bf16[32,2,3840]{2,1,0:T(2,128)(2,1)} %reshape.1044), calls=%async_computation.11 | async-start | bytes 983040 | tf_op jit(solution)/shard_map/all_to_all | solution.py:196
  923.8 195.7 %reduce-scatter.9.cloned.1.call-start = ((), (), s32[]{:S(2)}) async-start(), calls=%async_computation.21 | async-start | bytes 202752
  926.0 14.6 copy-start.119
  926.0 14.6 copy-start.122
  926.0 14.6 copy-start.132
  926.0 14.6 copy-start.143
  926.0 14.6 copy-start.147
  926.0 14.6 copy-start.151
  926.0 14.6 copy-start.154
  926.1 225.1 %all-reduce.29.cloned.1.call-start = ((), (), s32[]{:S(2)}) async-start(), calls=%async_computation.17 | async-start | bytes 1572864 | tf_op jit(solution)/shard_map/psum | solution.py:249
  956.9 163.9 %copy-start.62 = (bf16[6,64,256]{2,1,0:T(8,128)(2,1)S(1)}, bf16[6,64,256]{2,1,0:T(8,128)(2,1)}, u32[]{:S(2)}) copy-start(bf16[6,64,256]{2,1,0:T(8,128)(2,1)} %copy-done.61) | copy-start | bytes 589828
  956.9 402.2 %reduce-scatter.7.cloned.1.call-start = ((), (), s32[]{:S(2)}) async-start(), calls=%async_computation.20 | async-start | bytes 608256
  960.1 163.9 %copy-start.57 = (bf16[320,768]{1,0:T(8,128)(2,1)S(1)}, bf16[320,768]{1,0:T(8,128)(2,1)}, u32[]{:S(2)}) copy-start(bf16[320,768]{1,0:T(8,128)(2,1)} %reshape.988) | copy-start | bytes 1474564
  1123.6 593.4 %all-reduce.31.cloned.1.call-start = ((), (), s32[]{:S(2)}) async-start(), calls=%async_computation.19 | async-start | bytes 4718592
  1151.1 95.8 %copy-start.165 = (f32[256]{0:T(256)S(1)}, f32[256]{0:T(256)}, u32[]{:S(2)}) copy-start(f32[256]{0:T(256)} %get-tuple-element.125) | copy-start | bytes 3076
  (158 other events, 494.6 us)
Sparse Core Ops, SparseCore 0:
  11.1 72.6 all-gather.6
  219.6 20.1 all-reduce.22
  431.5 18.6 all-reduce.24
  625.9 25.8 all-reduce.32
  815.7 22.5 all-reduce.26
  928.9 190.5 reduce-scatter.8
  1122.0 21.8 all-reduce.28
  1149.5 209.5 reduce-scatter.6
  1361.7 355.2 all-reduce.30
where the time goes:
time: 1740 us; the launch traced here: 1730 us
  waiting for transfers between devices  765 us (44%)
  blocking collectives  436 us (25%)
  matrix products  175 us (10%)
  local copies, waits for them, and re-layouts  147 us (8%)
  other arithmetic  99.6 us (6%)
  starting transfers between devices  84.6 us (5%)
  between operations  17.5 us (1%)
    unnamed x12, waiting for transfers between devices  626 us
    unnamed x2, blocking collectives  190 us
    all_gather x1, blocking collectives, local(): lax.all_gather(router_weight[0], 'dp', axis=0, tiled=True)  96.3 us
    all_gather x1, blocking collectives, local(): lax.all_gather(out_weight[0], 'dp', axis=1, tiled=True)  90.4 us
    unnamed x383, local copies, waits for them, and re-layouts  60.7 us
    psum x3, waiting for transfers between devices, layer_forward(): attention = lax.psum(partial_attn, 'tensor')  41.7 us
  transfers between devices with their start and end apart: 24, of which 19 were waited for; matrix products, arithmetic and copies ran while one was open for 12% of the time, Pallas kernels for 0%

commit v1 on v0

v1 whole, which is shorter than its diff:
```python
import jax
import jax.numpy as jnp
from jax import lax
from jax.sharding import PartitionSpec as P

HEAD_DIM = 64
EPS = 1e-06
MASK_FILL = -1e30
SLOT_ROWS = 8

F32 = jnp.float32
BF16 = jnp.bfloat16


def swap(value, axis):
    return lax.ppermute(value, axis, [(0, 1), (1, 0)])


def dot(left, right, dims):
    return lax.dot_general(left, right, (dims, ((), ())), preferred_element_type=F32)


def rms_parts(rows_in, gain_row):
    inv_scale = lax.rsqrt(jnp.mean(rows_in * rows_in, axis=-1, keepdims=True) + EPS)
    normed = rows_in * inv_scale
    return (inv_scale, normed, (normed * gain_row).astype(BF16))


def rms_back(grad_out, inv_scale, normed, gain_row):
    grad_normed = grad_out * gain_row
    gain_grad = jnp.sum(grad_out * normed, axis=0)
    grad_in = inv_scale * (
        grad_normed - normed * jnp.mean(grad_normed * normed, axis=-1, keepdims=True)
    )
    return (grad_in, gain_grad)


def gelu_tanh(values):
    return jax.nn.gelu(values, approximate=True)


def pack_shard(qkv, out, router, attn_gain, moe_gain):
    owned, local_width = qkv.shape[1:]
    small = jnp.concatenate([router.reshape(-1), attn_gain, moe_gain])
    small = jnp.pad(small, (0, 8 * local_width - small.shape[0])).reshape(8, local_width)
    return jnp.concatenate([qkv.reshape(3 * owned, local_width), out.T, small], axis=0)


def unpack_dense(blocks, experts):
    parts, _, local_width = blocks.shape
    owned = 24
    qkv = blocks[:, : 3 * owned].reshape(parts, 3, owned, local_width)
    qkv = qkv.transpose(1, 0, 2, 3).reshape(3, parts * owned, local_width)
    out_t = blocks[:, 3 * owned : 4 * owned].reshape(parts * owned, local_width)
    small = blocks[:, 4 * owned :].reshape(parts, 8 * local_width)
    count = owned * experts
    router = small[:, :count].reshape(parts * owned, experts)
    attn_gain = small[:, count : count + owned].reshape(parts * owned).astype(F32)
    moe_gain = small[:, count + owned : count + 2 * owned].reshape(parts * owned).astype(F32)
    return (attn_gain, moe_gain, qkv, out_t, router)


def pack_grads(grads, parts):
    attn_gain_grad, moe_gain_grad, qkv_grad, out_grad_t, router_grad = grads
    model_width, local_width = out_grad_t.shape
    owned = model_width // parts
    qkv = qkv_grad.astype(BF16).reshape(3, parts, owned, local_width).transpose(1, 0, 2, 3)
    small = jnp.concatenate(
        [
            router_grad.reshape(parts, -1),
            attn_gain_grad.reshape(parts, owned),
            moe_gain_grad.reshape(parts, owned),
        ],
        axis=1,
    ).astype(BF16)
    small = jnp.pad(small, ((0, 0), (0, 8 * local_width - small.shape[1])))
    return jnp.concatenate(
        [
            qkv.reshape(parts, 3 * owned, local_width),
            out_grad_t.astype(BF16).reshape(parts, owned, local_width),
            small.reshape(parts, 8, local_width),
        ],
        axis=1,
    )


def slot_masks(route_row, keep_row, experts, capacity, core):
    chosen = (route_row[:, None] == jnp.arange(experts, dtype=jnp.int32)[None, :]).astype(F32)
    kept_hot = chosen * keep_row[:, None].astype(F32)
    count = route_row.shape[0]
    earlier = (jnp.arange(count)[:, None] > jnp.arange(count)[None, :]).astype(BF16)
    before = dot(earlier, kept_hot.astype(BF16), ((1,), (0,)))
    rank_row = jnp.sum(before * kept_hot, axis=1).astype(jnp.int32)
    half = capacity // 2
    slot = route_row * SLOT_ROWS + rank_row % half
    slot = jnp.where(keep_row == 1, slot, -1)
    in_half = rank_row // half
    columns = jnp.arange(experts * SLOT_ROWS, dtype=jnp.int32)[None, :]
    placed = slot[:, None] == columns
    own = (placed & (in_half == core)[:, None]).astype(BF16)
    other = (placed & (in_half == 1 - core)[:, None]).astype(BF16)
    return (chosen, own, other)


def head_scores(queries, key_rows, seg_row):
    scores = jnp.einsum(
        "qhe,khe->hqk", queries, key_rows, preferred_element_type=F32
    ) * HEAD_DIM ** (-0.5)
    same_doc = (seg_row[:, None] == seg_row[None, :])[None]
    return (scores, same_doc)


def attention_forward(hidden_in, seg_row, dense_full):
    attn_gain, moe_gain, qkv_full, out_t, router_full = dense_full
    row_count = hidden_in.shape[0]
    local_width = qkv_full.shape[2]
    head_count = local_width // HEAD_DIM
    scale_one, normed_one, normed_low = rms_parts(hidden_in, attn_gain)
    qkv_rows = jnp.einsum(
        "sd,cde->cse", normed_low, qkv_full, preferred_element_type=F32
    ).astype(BF16)
    queries = qkv_rows[0].reshape(row_count, head_count, HEAD_DIM)
    key_rows = qkv_rows[1].reshape(row_count, head_count, HEAD_DIM)
    value_rows = qkv_rows[2].reshape(row_count, head_count, HEAD_DIM)
    scores, same_doc = head_scores(queries, key_rows, seg_row)
    masked = jnp.where(same_doc, scores, MASK_FILL)
    row_max = jnp.max(masked, axis=-1, keepdims=True)
    exponent = jnp.exp(masked - row_max)
    row_total = jnp.sum(exponent, axis=-1, keepdims=True)
    soft_rows = (exponent / row_total).astype(BF16)
    log_total = row_max + jnp.log(row_total)
    mixed_heads = (
        jnp.einsum("hqk,khe->qhe", soft_rows, value_rows, preferred_element_type=F32)
        .astype(BF16)
        .reshape(row_count, local_width)
    )
    partial_attn = dot(mixed_heads, out_t, ((1,), (1,)))
    hidden = hidden_in + (partial_attn + swap(partial_attn, "tensor"))
    scale_two, normed_two, moe_in = rms_parts(hidden, moe_gain)
    logits = dot(moe_in, router_full, ((1,), (0,)))
    router_prob = jax.nn.softmax(logits, axis=-1)
    saved = (
        normed_low,
        scale_one,
        normed_one,
        queries,
        key_rows,
        value_rows,
        log_total,
        mixed_heads,
        scale_two,
        normed_two,
        moe_in,
        router_prob,
    )
    return (hidden, moe_in, router_prob, saved)


def attention_backward(grad_out, grad_back, grad_gate, gate_prob, chosen, saved, seg_row, dense_full):
    (
        normed_low,
        scale_one,
        normed_one,
        queries,
        key_rows,
        value_rows,
        log_total,
        mixed_heads,
        scale_two,
        normed_two,
        moe_in,
        router_prob,
    ) = saved
    attn_gain, moe_gain, qkv_full, out_t, router_full = dense_full
    row_count = grad_out.shape[0]
    local_width = qkv_full.shape[2]
    head_count = local_width // HEAD_DIM
    scaling = HEAD_DIM ** (-0.5)
    grad_logits = ((grad_gate * gate_prob)[:, None] * (chosen - router_prob)).astype(BF16)
    router_grad = dot(moe_in, grad_logits, ((0,), (0,)))
    grad_moe_in = grad_back + dot(grad_logits, router_full, ((1,), (1,)))
    grad_norm_two, moe_gain_grad = rms_back(grad_moe_in, scale_two, normed_two, moe_gain)
    grad_hidden = grad_out + grad_norm_two
    grad_attention = grad_hidden.astype(BF16)
    out_grad_t = dot(grad_attention, mixed_heads, ((0,), (0,)))
    grad_mixed = (
        dot(grad_attention, out_t, ((1,), (0,)))
        .astype(BF16)
        .reshape(row_count, head_count, HEAD_DIM)
    )
    scores, same_doc = head_scores(queries, key_rows, seg_row)
    soft_rows = jnp.where(same_doc, jnp.exp(scores - log_total), 0.0)
    grad_soft = jnp.einsum("qhe,khe->hqk", grad_mixed, value_rows, preferred_element_type=F32)
    row_delta = jnp.sum(soft_rows * grad_soft, axis=-1, keepdims=True)
    grad_scores = (soft_rows * (grad_soft - row_delta)).astype(BF16)
    grad_values = jnp.einsum(
        "hqk,qhe->khe", soft_rows.astype(BF16), grad_mixed, preferred_element_type=F32
    )
    grad_queries = (
        jnp.einsum("hqk,khe->qhe", grad_scores, key_rows, preferred_element_type=F32) * scaling
    )
    grad_keys = (
        jnp.einsum("hqk,qhe->khe", grad_scores, queries, preferred_element_type=F32) * scaling
    )
    grad_qkv = (
        jnp.stack([grad_queries, grad_keys, grad_values])
        .astype(BF16)
        .reshape(3, row_count, local_width)
    )
    qkv_grad = jnp.einsum("sd,cse->cde", normed_low, grad_qkv, preferred_element_type=F32)
    partial_norm = jnp.einsum("cse,cde->sd", grad_qkv, qkv_full, preferred_element_type=F32)
    grad_normed = partial_norm + swap(partial_norm, "tensor")
    grad_norm_one, attn_gain_grad = rms_back(grad_normed, scale_one, normed_one, attn_gain)
    grad_in = grad_hidden + grad_norm_one
    return (grad_in, (attn_gain_grad, moe_gain_grad, qkv_grad, out_grad_t, router_grad))


def to_experts(rows):
    doubled = jnp.concatenate([rows, rows], axis=0)
    return lax.all_to_all(doubled, ("section", "dp"), split_axis=0, concat_axis=0, tiled=True)


def from_experts(blocks, layer):
    arrived = lax.all_to_all(blocks, ("section", "dp"), split_axis=0, concat_axis=0, tiled=True)
    experts = blocks.shape[0] // 2
    return arrived[layer * experts : (layer + 1) * experts]


def to_slots(mask, rows, experts):
    return dot(mask, rows, ((0,), (0,))).astype(BF16).reshape(experts, SLOT_ROWS, rows.shape[1])


def to_tokens(own, other, slot_rows):
    flat = slot_rows.reshape(-1, slot_rows.shape[-1])
    return dot(own, flat, ((1,), (0,))) + dot(other, swap(flat, "tensor"), ((1,), (0,)))


def expert_forward(rows, halves_in, halves_out):
    hidden = [dot(rows, half, ((1,), (0,))) for half in halves_in]
    total = 0.0
    for part, half in zip(hidden, halves_out):
        total = total + dot(gelu_tanh(part).astype(BF16), half, ((1,), (0,)))
    return (hidden, total.astype(BF16))


def expert_backward(hidden, grad_rows, halves_in, halves_out):
    total = 0.0
    for part, half_in, half_out in zip(hidden, halves_in, halves_out):
        grad_act = dot(grad_rows, half_out, ((1,), (1,)))
        grad_pre = jax.vjp(gelu_tanh, part)[1](grad_act)[0].astype(BF16)
        total = total + dot(grad_pre, half_in, ((1,), (1,)))
    return total.astype(BF16)


def expert_weight_grads(rows, grad_rows, half_in, half_out):
    hidden = dot(rows, half_in, ((1,), (0,)))
    activated = gelu_tanh(hidden).astype(BF16)
    grad_act = dot(grad_rows, half_out, ((1,), (1,)))
    grad_pre = jax.vjp(gelu_tanh, hidden)[1](grad_act)[0].astype(BF16)
    return (dot(rows, grad_pre, ((0,), (0,))), dot(activated, grad_rows, ((0,), (0,))))


def local(
    tokens,
    cotangent,
    segments,
    routes,
    keeps,
    attn_gain,
    moe_gain,
    qkv_weight,
    out_weight,
    router_weight,
    expert_in,
    expert_out,
):
    section = lax.axis_index("section")
    core = lax.axis_index("tensor")
    first = section == 0
    _, seq_len = segments.shape
    model_width = tokens.shape[1]
    experts = router_weight.shape[2]
    parts = lax.axis_size("dp")
    capacity = max(2, 5 * seq_len // (4 * experts))

    mine = pack_shard(
        qkv_weight[0], out_weight[0], router_weight[0], attn_gain[0], moe_gain[0]
    )
    theirs = swap(mine, "section")
    shard_zero = jnp.where(first, mine, theirs)
    shard_one = jnp.where(first, theirs, mine)
    blocks_zero = lax.all_to_all(
        jnp.broadcast_to(shard_zero[None], (parts,) + shard_zero.shape),
        "dp",
        split_axis=0,
        concat_axis=0,
        tiled=True,
    )
    blocks_one = lax.all_gather(shard_one, "dp", axis=0, tiled=False)
    dense_zero = unpack_dense(blocks_zero, experts)
    dense_one = unpack_dense(blocks_one, experts)

    half_in = expert_in[0, 0]
    half_out = expert_out[0, 0]
    halves_in = (half_in, swap(half_in, "tensor"))
    halves_out = (half_out, swap(half_out, "tensor"))

    hidden_in = lax.dynamic_slice_in_dim(tokens, section * seq_len, seq_len, 0).astype(F32)
    target = lax.dynamic_slice_in_dim(cotangent, section * seq_len, seq_len, 0).astype(F32)
    seg_row = jnp.where(first, segments[0], segments[1])
    coded = (routes[0] + experts * keeps[0]).reshape(2, seq_len)
    coded_own = jnp.where(first, coded[0], coded[1])
    coded_other = swap(jnp.where(first, coded[1], coded[0]), "section")
    masks = []
    for code in (
        jnp.where(first, coded_own, coded_other),
        jnp.where(first, coded_other, coded_own),
    ):
        masks.append(slot_masks(code % experts, code // experts, experts, capacity, core))

    chosen_zero, own_zero, other_zero = masks[0]
    hidden_zero, moe_zero, prob_zero, saved_zero = attention_forward(
        hidden_in, seg_row, dense_zero
    )
    gate_zero = jnp.sum(prob_zero * chosen_zero, axis=1)
    arrived_zero = to_experts(to_slots(own_zero, moe_zero, experts))
    rows_zero = arrived_zero.reshape(-1, model_width)
    pre_zero, result_zero = expert_forward(rows_zero, halves_in, halves_out)
    returned_zero = to_tokens(
        own_zero, other_zero, from_experts(result_zero.reshape(arrived_zero.shape), 0)
    )
    layer_zero = hidden_zero + gate_zero[:, None] * returned_zero

    chosen_one, own_one, other_one = masks[1]
    hidden_one, moe_one, prob_one, saved_one = attention_forward(layer_zero, seg_row, dense_one)
    gate_one = jnp.sum(prob_one * chosen_one, axis=1)
    grad_tokens = (gate_one[:, None] * target).astype(BF16)
    arrived_one = to_experts(
        jnp.concatenate(
            [to_slots(own_one, moe_one, experts), to_slots(own_one, grad_tokens, experts)], axis=1
        )
    )
    rows_one = arrived_one[:, :SLOT_ROWS].reshape(-1, model_width)
    grad_rows_one = arrived_one[:, SLOT_ROWS:].reshape(-1, model_width)
    pre_one, result_one = expert_forward(rows_one, halves_in, halves_out)
    grad_x_one = expert_backward(pre_one, grad_rows_one, halves_in, halves_out)
    back_one = from_experts(
        jnp.concatenate(
            [
                result_one.reshape(-1, SLOT_ROWS, model_width),
                grad_x_one.reshape(-1, SLOT_ROWS, model_width),
            ],
            axis=1,
        ),
        1,
    )
    returned_one = to_tokens(own_one, other_one, back_one[:, :SLOT_ROWS])
    layer_one = hidden_one + gate_one[:, None] * returned_one
    grad_back_one = to_tokens(own_one, other_one, back_one[:, SLOT_ROWS:])

    grad_gate_one = jnp.sum(target * returned_one, axis=1)
    grad_mid, grads_one = attention_backward(
        target,
        grad_back_one,
        grad_gate_one,
        gate_one,
        chosen_one,
        saved_one,
        seg_row,
        dense_one,
    )

    grad_tokens = (gate_zero[:, None] * grad_mid).astype(BF16)
    grad_gate_zero = jnp.sum(grad_mid * returned_zero, axis=1)
    grad_rows_zero = to_experts(to_slots(own_zero, grad_tokens, experts)).reshape(-1, model_width)
    grad_x_zero = expert_backward(pre_zero, grad_rows_zero, halves_in, halves_out)
    grad_back_zero = to_tokens(
        own_zero, other_zero, from_experts(grad_x_zero.reshape(-1, SLOT_ROWS, model_width), 0)
    )
    grad_first, grads_zero = attention_backward(
        grad_mid,
        grad_back_zero,
        grad_gate_zero,
        gate_zero,
        chosen_zero,
        saved_zero,
        seg_row,
        dense_zero,
    )

    rows_own = jnp.where(first, rows_zero, rows_one)
    grad_rows_own = jnp.where(first, grad_rows_zero, grad_rows_one)
    expert_in_grad, expert_out_grad = expert_weight_grads(
        jnp.concatenate([rows_own, swap(rows_own, "tensor")], axis=0),
        jnp.concatenate([grad_rows_own, swap(grad_rows_own, "tensor")], axis=0),
        half_in,
        half_out,
    )

    sums = []
    for grads in (grads_zero, grads_one):
        pieces = lax.all_to_all(
            pack_grads(grads, parts), "dp", split_axis=0, concat_axis=0, tiled=True
        )
        sums.append(jnp.sum(pieces.astype(F32), axis=0))
    owned = jnp.where(first, sums[0], sums[1]) + swap(
        jnp.where(first, sums[1], sums[0]), "section"
    )
    width = owned.shape[1]
    share = model_width // parts
    qkv_grad = owned[: 3 * share].reshape(3, share, width)
    out_grad = owned[3 * share : 4 * share].T
    small = owned[4 * share :].reshape(-1)
    count = share * experts
    router_grad = small[:count].reshape(share, experts)
    attn_gain_grad = small[count : count + share]
    moe_gain_grad = small[count + share : count + 2 * share]

    def settle(of_zero, of_one):
        offset = core * width
        of_zero = lax.dynamic_slice_in_dim(of_zero, offset, width, 1)
        of_one = lax.dynamic_slice_in_dim(of_one, offset, width, 1)
        kept = jnp.where(first, of_zero, of_one)
        came = swap(jnp.where(first, of_one, of_zero), "section")
        return jnp.concatenate(
            [jnp.where(first, kept, came), jnp.where(first, came, kept)], axis=0
        )[None]

    return (
        settle(layer_zero, layer_one),
        settle(grad_first, grad_mid),
        attn_gain_grad[None],
        moe_gain_grad[None],
        qkv_grad[None],
        out_grad[None],
        router_grad[None],
        expert_in_grad[None, None],
        expert_out_grad[None, None],
    )


def solution(mesh):
    placed = (
        P("dp", None),
        P("dp", None),
        P("dp", None),
        P("section", "dp"),
        P("section", "dp"),
        P("section", "dp"),
        P("section", "dp"),
        P("section", None, "dp", "tensor"),
        P("section", "tensor", "dp"),
        P("section", "dp", None),
        P("section", "dp", None, "tensor"),
        P("section", "dp", "tensor", None),
    )
    return jax.shard_map(
        local,
        mesh=mesh,
        in_specs=placed,
        out_specs=(
            P("section", "dp", "tensor"),
            P("section", "dp", "tensor"),
            P("section", "dp"),
            P("section", "dp"),
            P("section", None, "dp", "tensor"),
            P("section", "tensor", "dp"),
            P("section", "dp", None),
            P("section", "dp", None, "tensor"),
            P("section", "dp", "tensor", None),
        ),
        check_vma=False,
    )
```

time: 1740 us -> 489 us (0.28)
  the two profiles are of different devices: /device:TPU:0 before, /device:TPU:19 now
where the time goes in v1:
time: 489 us; the launch traced here: 481 us
  matrix products  132 us (27%)
  waiting for transfers between devices  103 us (21%)
  starting transfers between devices  81.9 us (17%)
  local copies, waits for them, and re-layouts  55 us (11%)
  blocking collectives  52.8 us (11%)
  other arithmetic  40 us (8%)
  between operations  16.2 us (3%)
    dot_general x41, matrix products, dot(): lax.dot_general(left, right, (dims, ((), ())), preferred_element_type=F32)  109 us
    all_to_all x2, blocking collectives, to_experts(): lax.all_to_all(doubled, ('section', 'dp'), split_axis=0, concat_axis=0, t...  52.8 us
    ppermute x17, waiting for transfers between devices, swap(): return lax.ppermute(value, axis, [(0, 1), (1, 0)])  47.3 us
    all_to_all x3, waiting for transfers between devices, from_experts(): lax.all_to_all(blocks, ('section', 'dp'), split_axis=0, concat_axis=0, ti...  36.6 us
    all_to_all x3, starting transfers between devices, from_experts(): lax.all_to_all(blocks, ('section', 'dp'), split_axis=0, concat_axis=0, ti...  25 us
    ppermute x17, starting transfers between devices, swap(): return lax.ppermute(value, axis, [(0, 1), (1, 0)])  22.8 us
    all_to_all x2, starting transfers between devices, local(): lax.all_to_all(pack_grads(grads, parts), 'dp', split_axis=0, concat_axis=...  16.2 us
    all_gather x1, waiting for transfers between devices, local(): blocks_one = lax.all_gather(shard_one, 'dp', axis=0, tiled=False)  10.6 us
  transfers between devices with their start and end apart: 25, of which 11 were waited for; matrix products, arithmetic and copies ran while one was open for 27% of the time, Pallas kernels for 0%

profile of v1, /device:TPU:19, one launch (start us, length us, event | category | flops | bytes accessed | tf_op | source)
XLA Modules:
  0.0 481.0 jit_solution(18211800480977996159)
XLA Ops:
  10.6 2.3 collective-permute-done
  16.1 10.5 %all-to-all-start = ((bf16[32,104,384]{2,1,0:T(8,128)(2,1)}), bf16[32,104,384]{2,1,0:T(8,128)(2,1)}, u32[]{:S(2)}, u32[]{:S(2)}) async-start(bf16[32,104,384]{2,1,0:T(8,128)(2,1)} %broadcast_in_dim.45), calls=%async_computation | async-start | bytes 5111808 | tf_op jit(solution)/shard_map/all_to_all | solution.py:292
  27.8 2.7 collective-permute-start.4
  30.8 29.4 %collective-permute-done.2 = s32[256]{0:T(256)S(1)} collective-permute-done((s32[256]{0:T(256)S(1)}, s32[256]{0:T(256)S(1)}, u32[]{:S(2)}, u32[]{:S(2)}) %collective-permute-start.2) | collective-permute-done | bytes 1056 | tf_op jit(solution)/shard_map/ppermute | solution.py:16
  77.5 22.3 %all_to_all.45 = bf16[64,8,768]{2,1,0:T(8,128)(2,1)S(1)} all-to-all(bf16[64,8,768]{2,1,0:T(8,128)(2,1)S(1)} %pad_maximum_fusion.13), channel_id=1, replica_groups=mesh['section'=2,'dp'=32,'tensor'=2] {'section','dp'}, dimensions={0} | all-to-all | bytes 1572864 | tf_op jit(solution)/shard_map/all_to_all | solution.py:220
  101.2 4.2 fusion.98
  107.4 4.5 fusion.61
  112.0 7.1 %all-to-all-start.2 = ((bf16[64,8,768]{2,1,0:T(8,128)(2,1)}), bf16[64,8,768]{2,1,0:T(8,128)(2,1)}, u32[]{:S(2)}, u32[]{:S(2)}) async-start(bf16[64,8,768]{2,1,0:T(8,128)(2,1)} %fusion.61), calls=%async_computation.2 | async-start | bytes 1572864 | tf_op jit(solution)/shard_map/all_to_all | solution.py:224
  119.7 10.8 %all-to-all-done.2 = bf16[64,8,768]{2,1,0:T(8,128)(2,1)} async-done(((bf16[64,8,768]{2,1,0:T(8,128)(2,1)}), bf16[64,8,768]{2,1,0:T(8,128)(2,1)}, u32[]{:S(2)}, u32[]{:S(2)}) %all-to-all-start.2) | async-done | bytes 786464 | tf_op jit(solution)/shard_map/all_to_all | solution.py:224
  132.3 3.0 collective-permute-start.5
  136.7 10.6 %all-gather.3.cloned.1.call-done = bf16[3328,384]{1,0:T(8,128)(2,1)} async-done(((bf16[104,384]{1,0:T(8,128)(2,1)}), bf16[3328,384]{1,0:T(8,128)(2,1)}) %all-gather.3.cloned.1.call-update) | async-done | bytes 2555920 | tf_op jit(solution)/shard_map/all_gather | solution.py:299
  154.2 2.4 multiply_reduce_fusion.12
  169.0 30.5 %all_to_all.46 = bf16[64,16,768]{2,1,0:T(8,128)(2,1)S(1)} all-to-all(bf16[64,16,768]{2,1,0:T(8,128)(2,1)S(1)} %maximum_maximum_fusion), channel_id=1, replica_groups=mesh['section'=2,'dp'=32,'tensor'=2] {'section','dp'}, dimensions={0} | all-to-all | bytes 3145728 | tf_op jit(solution)/shard_map/all_to_all | solution.py:220
  203.8 3.1 fusion.41
  206.9 8.2 %fusion.45 = f32[512,768]{1,0:T(8,128)} fusion(f32[512,1536]{1,0:T(8,128)} %copy-done.97, bf16[64,16,768]{2,1,0:T(8,128)(2,1)} %copy-done.13, bf16[1,1,1536,768]{3,2,1,0:T(8,128)(2,1)} %param.23, bf16[1,1,768,1536]{3,2,1,0:T(8,128)(2,1)} %param.22), kind=kOutput, calls=%fused_computation.84 | convolution fusion | flops 2431647744 | bytes 10223616 | tf_op jit(solution)/shard_map/dot_general | solution.py:20
  215.1 5.0 %fusion.108 = f32[512,1536]{1,0:T(8,128)} fusion(bf16[768,1536]{1,0:T(8,128)(2,1)} %collective-permute-done.3, bf16[64,16,768]{2,1,0:T(8,128)(2,1)} %copy-done.13), kind=kOutput, calls=%fused_computation.195 | convolution fusion | flops 1207959552 | bytes 6291456 | tf_op jit(solution)/shard_map/dot_general | solution.py:20
  220.1 8.4 %fusion.55 = bf16[64,8,768]{2,1,0:T(8,128)(2,1)} fusion(f32[512,768]{1,0:T(8,128)} %fusion.45, bf16[768,1536]{1,0:T(8,128)(2,1)} %collective-permute-done.3, f32[512,1536]{1,0:T(8,128)} %fusion.108, bf16[1536,768]{1,0:T(8,128)(2,1)} %collective-permute-done.4, bf16[64,16,768]{2,1,0:T(8,128)(2,1)} %copy-done.13), kind=kOutput, calls=%fused_computation.95 | convolution fusion | flops 2432434176 | bytes 11010048 | tf_op jit(solution)/shard_map/dot_general | solution.py:20
  228.5 5.1 %fusion.62 = bf16[64,8,768]{2,1,0:T(8,128)(2,1)S(1)} fusion(f32[512,768]{1,0:T(8,128)} %fusion.41, bf16[1536,768]{1,0:T(8,128)(2,1)} %collective-permute-done.4, f32[512,1536]{1,0:T(8,128)} %fusion.108), kind=kOutput, calls=%fused_computation.98 | convolution fusion | flops 1215823872 | bytes 7864320 | tf_op jit(solution)/shard_map/dot_general | solution.py:20
  234.9 7.6 %all-to-all-start.4 = ((bf16[64,16,768]{2,1,0:T(8,128)(2,1)}), bf16[64,16,768]{2,1,0:T(8,128)(2,1)}, u32[]{:S(2)}, u32[]{:S(2)}) async-start(bf16[64,16,768]{2,1,0:T(8,128)(2,1)} %pad_maximum_fusion.2), calls=%async_computation.4 | async-start | bytes 3145728 | tf_op jit(solution)/shard_map/all_to_all | solution.py:224
  242.5 19.9 %all-to-all-done.4 = bf16[64,16,768]{2,1,0:T(8,128)(2,1)} async-done(((bf16[64,16,768]{2,1,0:T(8,128)(2,1)}), bf16[64,16,768]{2,1,0:T(8,128)(2,1)}, u32[]{:S(2)}, u32[]{:S(2)}) %all-to-all-start.4) | async-done | bytes 1572896 | tf_op jit(solution)/shard_map/all_to_all | solution.py:224
  263.6 3.0 collective-permute-start.7
  283.0 2.5 convolution_bitcast_fusion.3
  286.0 3.1 convert_bitcast_fusion
  295.6 7.5 %all-to-all-start.5 = ((bf16[64,8,768]{2,1,0:T(8,128)(2,1)}), bf16[64,8,768]{2,1,0:T(8,128)(2,1)}, u32[]{:S(2)}, u32[]{:S(2)}) async-start(bf16[64,8,768]{2,1,0:T(8,128)(2,1)} %pad_maximum_fusion.14), calls=%async_computation.5 | async-start | bytes 1572864 | tf_op jit(solution)/shard_map/all_to_all | solution.py:220
  308.0 3.9 copy.68
  311.9 3.0 copy.69
  315.3 6.2 %collective-permute-done.8 = f32[256,384]{1,0:T(8,128)} collective-permute-done((f32[256,384]{1,0:T(8,128)}, f32[256,384]{1,0:T(8,128)}, u32[]{:S(2)}, u32[]{:S(2)}) %collective-permute-start.8) | collective-permute-done | bytes 393248 | tf_op jit(solution)/shard_map/ppermute | solution.py:16
  323.5 8.2 %fusion.49 = f32[512,768]{1,0:T(8,128)} fusion(f32[512,1536]{1,0:T(8,128)} %copy-done.95, bf16[64,8,768]{2,1,0:T(8,128)(2,1)} %all-to-all-done.5, bf16[1,1,1536,768]{3,2,1,0:T(8,128)(2,1)} %param.23, bf16[1,1,768,1536]{3,2,1,0:T(8,128)(2,1)} %param.22), kind=kOutput, calls=%fused_computation.86 | convolution fusion | flops 2431647744 | bytes 10223616 | tf_op jit(solution)/shard_map/dot_general | solution.py:20
  331.7 8.4 %fusion.58 = bf16[64,8,768]{2,1,0:T(8,128)(2,1)} fusion(f32[512,768]{1,0:T(8,128)} %fusion.49, bf16[768,1536]{1,0:T(8,128)(2,1)} %collective-permute-done.3, f32[512,1536]{1,0:T(8,128)} %copy-done.96, bf16[1536,768]{1,0:T(8,128)(2,1)} %collective-permute-done.4, bf16[64,8,768]{2,1,0:T(8,128)(2,1)} %all-to-all-done.5), kind=kOutput, calls=%fused_computation.96 | convolution fusion | flops 2432434176 | bytes 11010048 | tf_op jit(solution)/shard_map/dot_general | solution.py:20
  340.2 10.3 %all-to-all-start.6 = ((bf16[64,8,768]{2,1,0:T(8,128)(2,1)}), bf16[64,8,768]{2,1,0:T(8,128)(2,1)}, u32[]{:S(2)}, u32[]{:S(2)}) async-start(bf16[64,8,768]{2,1,0:T(8,128)(2,1)} %fusion.58), calls=%async_computation.6 | async-start | bytes 1572864 | tf_op jit(solution)/shard_map/all_to_all | solution.py:224
  353.8 3.2 pad_maximum_fusion.1
  357.0 6.0 %all-to-all-done.6 = bf16[64,8,768]{2,1,0:T(8,128)(2,1)} async-done(((bf16[64,8,768]{2,1,0:T(8,128)(2,1)}), bf16[64,8,768]{2,1,0:T(8,128)(2,1)}, u32[]{:S(2)}, u32[]{:S(2)}) %all-to-all-start.6) | async-done | bytes 786464 | tf_op jit(solution)/shard_map/all_to_all | solution.py:224
  363.0 6.4 %all-to-all-start.8 = ((bf16[32,104,384]{2,1,0:T(8,128)(2,1)}), bf16[32,104,384]{2,1,0:T(8,128)(2,1)}, u32[]{:S(2)}, u32[]{:S(2)}) async-start(bf16[32,104,384]{2,1,0:T(8,128)(2,1)} %pad_maximum_fusion.1), calls=%async_computation.8 | async-start | bytes 5111808 | tf_op jit(solution)/shard_map/all_to_all | solution.py:402
  370.4 2.7 collective-permute-start.11
  373.1 2.7 bitcast_select_fusion
  388.8 2.3 convolution_bitcast_fusion.2
  391.4 6.2 %fusion.80 = f32[1024,1536]{1,0:T(8,128)} fusion(bf16[512,768]{1,0:T(8,128)(2,1)} %collective-permute-done.15, bf16[512,768]{1,0:T(8,128)(2,1)} %get-tuple-element.39, bf16[1,1,768,1536]{3,2,1,0:T(8,128)(2,1)S(1)} %copy-done.92), kind=kOutput, calls=%fused_computation.148 | convolution fusion | flops 2419064832 | bytes 10223616 | tf_op jit(solution)/shard_map/dot_general | solution.py:20
  398.5 2.9 convert_bitcast_fusion.1
  401.3 3.8 copy.64
  405.2 3.0 copy.65
  408.6 2.4 multiply_reduce_fusion.5
  411.2 3.2 pad_maximum_fusion
  414.4 9.8 %all-to-all-start.7 = ((bf16[32,104,384]{2,1,0:T(8,128)(2,1)}), bf16[32,104,384]{2,1,0:T(8,128)(2,1)}, u32[]{:S(2)}, u32[]{:S(2)}) async-start(bf16[32,104,384]{2,1,0:T(8,128)(2,1)} %pad_maximum_fusion), calls=%async_computation.7 | async-start | bytes 5111808 | tf_op jit(solution)/shard_map/all_to_all | solution.py:402
  424.2 9.0 %convolution_bitcast_fusion = f32[1,1,1536,768]{3,2,1,0:T(8,128)} fusion(f32[1024,1536]{1,0:T(8,128)} %fusion.80, bf16[512,768]{1,0:T(8,128)(2,1)} %collective-permute-done.16, bf16[512,768]{1,0:T(8,128)(2,1)} %get-tuple-element.38), kind=kOutput, calls=%fused_computation.20 | convolution fusion | flops 2433220608 | bytes 12582912 | tf_op jit(solution)/shard_map/dot_general | solution.py:20
  433.3 13.1 %convolution_bitcast_fusion.1 = f32[1,1,768,1536]{3,2,1,0:T(8,128)} fusion(f32[1024,1536]{1,0:T(8,128)} %fusion.80, bf16[512,768]{1,0:T(8,128)(2,1)} %collective-permute-done.16, bf16[512,768]{1,0:T(8,128)(2,1)} %get-tuple-element.38, bf16[512,768]{1,0:T(8,128)(2,1)} %collective-permute-done.15, bf16[512,768]{1,0:T(8,128)(2,1)} %get-tuple-element.39, ...), kind=kOutput, calls=%fused_computation.21 | convolution fusion | flops 4869586944 | bytes 16515072 | tf_op jit(solution)/shard_map/dot_general | solution.py:20
  450.3 8.7 %all-to-all-done.7 = bf16[32,104,384]{2,1,0:T(8,128)(2,1)} async-done(((bf16[32,104,384]{2,1,0:T(8,128)(2,1)}), bf16[32,104,384]{2,1,0:T(8,128)(2,1)}, u32[]{:S(2)}, u32[]{:S(2)}) %all-to-all-start.7) | async-done | bytes 2555936 | tf_op jit(solution)/shard_map/all_to_all | solution.py:402
  462.4 5.3 %collective-permute-done.13 = f32[256,384]{1,0:T(8,128)S(1)} collective-permute-done((f32[256,384]{1,0:T(8,128)S(1)}, f32[256,384]{1,0:T(8,128)S(1)}, u32[]{:S(2)}, u32[]{:S(2)}) %collective-permute-start.13) | collective-permute-done | bytes 393248 | tf_op jit(solution)/shard_map/ppermute | solution.py:16
  468.7 2.4 collective-permute-done.14
  (379 shorter events, 118.1 us)
Async XLA Ops:
  9.6 3.3 collective-permute-start
  16.1 14.4 %copy-start.37 = (bf16[512,768]{1,0:T(8,128)(2,1)S(1)}, bf16[512,768]{1,0:T(8,128)(2,1)}, u32[]{:S(2)}) copy-start(bf16[512,768]{1,0:T(8,128)(2,1)} %param.12) | copy-start | bytes 2359300
  16.1 44.1 %all-to-all-start = ((bf16[32,104,384]{2,1,0:T(8,128)(2,1)}), bf16[32,104,384]{2,1,0:T(8,128)(2,1)}, u32[]{:S(2)}, u32[]{:S(2)}) async-start(bf16[32,104,384]{2,1,0:T(8,128)(2,1)} %broadcast_in_dim.45), calls=%async_computation | async-start | bytes 5111808 | tf_op jit(solution)/shard_map/all_to_all | solution.py:292
  26.6 120.6 %all-gather.3.cloned.1.call-start = ((), (), s32[]{:S(2)}) async-start(), calls=%async_computation.9 | async-start | bytes 2635776 | tf_op jit(solution)/shard_map/all_gather | solution.py:299
  26.7 33.5 %collective-permute-start.2 = (s32[256]{0:T(256)S(1)}, s32[256]{0:T(256)S(1)}, u32[]{:S(2)}, u32[]{:S(2)}) collective-permute-start(s32[256]{0:T(256)S(1)} %bitcast.316), channel_id=1, source_target_pairs={{0,64},{64,0},{1,65},{65,1},{2,66},{66,2},{3,67},{67,3},{4,68},{68... | collective-permute-start | bytes 3080 | tf_op jit(solution)/shard_map/ppermute | solution.py:16
  27.8 79.6 %collective-permute-start.4 = (bf16[1536,768]{1,0:T(8,128)(2,1)}, bf16[1536,768]{1,0:T(8,128)(2,1)}, u32[]{:S(2)}, u32[]{:S(2)}) collective-permute-start(bf16[1536,768]{1,0:T(8,128)(2,1)} %bitcast.320), channel_id=1, source_target_pairs={{0,1},{1,0},{2,3},{3,2},{4,5},{5,4},{6,7},{7,6},{8,9},{9,8},{10,11... | collective-permute-start | bytes 7077896 | tf_op jit(solution)/shard_map/ppermute | solution.py:16
  30.5 70.7 %collective-permute-start.3 = (bf16[768,1536]{1,0:T(8,128)(2,1)}, bf16[768,1536]{1,0:T(8,128)(2,1)}, u32[]{:S(2)}, u32[]{:S(2)}) collective-permute-start(bf16[768,1536]{1,0:T(8,128)(2,1)} %bitcast.319), channel_id=1, source_target_pairs={{0,1},{1,0},{2,3},{3,2},{4,5},{5,4},{6,7},{7,6},{8,9},{9,8},{10,11... | collective-permute-start | bytes 7077896 | tf_op jit(solution)/shard_map/ppermute | solution.py:16
  30.8 33.8 %copy-start.77 = (f32[256]{0:T(256)}, f32[256]{0:T(256)S(1)}, u32[]{:S(2)}) copy-start(f32[256]{0:T(256)S(1)} %add_rsqrt_fusion.3) | copy-start | bytes 3076
  60.2 59.4 %copy-start.57 = (s32[256]{0:T(256)}, s32[256]{0:T(256)S(1)}, u32[]{:S(2)}) copy-start(s32[256]{0:T(256)S(1)} %get-tuple-element.64) | copy-start | bytes 3076
  60.2 103.3 %copy-start.59 = (s32[256]{0:T(256)}, s32[256]{0:T(256)S(1)}, u32[]{:S(2)}) copy-start(s32[256]{0:T(256)S(1)} %get-tuple-element.61) | copy-start | bytes 3076
  71.3 4.1 collective-permute-start.1
  73.6 80.6 %copy-start.84 = (pred[256]{0:T(512)(128)(4,1)}, pred[256]{0:T(512)(128)(4,1)S(1)}, u32[]{:S(2)}) copy-start(pred[256]{0:T(512)(128)(4,1)S(1)} %get-tuple-element.32) | copy-start | bytes 772
  73.6 61.8 %copy-start.72 = (pred[256]{0:T(512)(128)(4,1)}, pred[256]{0:T(512)(128)(4,1)S(1)}, u32[]{:S(2)}) copy-start(pred[256]{0:T(512)(128)(4,1)S(1)} %broadcast_compare_fusion.4) | copy-start | bytes 772
  76.8 77.3 %copy-start = (f32[256,768]{1,0:T(8,128)}, f32[256,768]{1,0:T(8,128)S(1)}, u32[]{:S(2)}) copy-start(f32[256,768]{1,0:T(8,128)S(1)} %get-tuple-element.35) | copy-start | bytes 2359300
  76.8 22.9 %copy-start.90 = (bf16[1,1,768,1536]{3,2,1,0:T(8,128)(2,1)S(1)}, bf16[1,1,768,1536]{3,2,1,0:T(8,128)(2,1)}, u32[]{:S(2)}) copy-start(bf16[1,1,768,1536]{3,2,1,0:T(8,128)(2,1)} %param.22) | copy-start | bytes 7077892
  76.9 24.3 %copy-start.63 = (f32[256]{0:T(256)}, f32[256]{0:T(256)S(1)}, u32[]{:S(2)}) copy-start(f32[256]{0:T(256)S(1)} %add_rsqrt_fusion.2) | copy-start | bytes 3076
  77.0 42.3 %copy-start.15 = (bf16[256,768]{1,0:T(8,128)(2,1)}, bf16[256,768]{1,0:T(8,128)(2,1)S(1)}, u32[]{:S(2)}) copy-start(bf16[256,768]{1,0:T(8,128)(2,1)S(1)} %multiply_convert_fusion.23) | copy-start | bytes 1179652
  112.0 18.5 %all-to-all-start.2 = ((bf16[64,8,768]{2,1,0:T(8,128)(2,1)}), bf16[64,8,768]{2,1,0:T(8,128)(2,1)}, u32[]{:S(2)}, u32[]{:S(2)}) async-start(bf16[64,8,768]{2,1,0:T(8,128)(2,1)} %fusion.61), calls=%async_computation.2 | async-start | bytes 1572864 | tf_op jit(solution)/shard_map/all_to_all | solution.py:224
  119.3 13.1 %copy-start.25 = (bf16[768,32]{1,0:T(8,128)(2,1)}, bf16[768,32]{1,0:T(8,128)(2,1)S(1)}, u32[]{:S(2)}) copy-start(bf16[768,32]{1,0:T(8,128)(2,1)S(1)} %reshape.401) | copy-start | bytes 147460
  119.6 29.3 %copy-start.61 = (f32[256]{0:T(256)}, f32[256]{0:T(256)S(1)}, u32[]{:S(2)}) copy-start(f32[256]{0:T(256)S(1)} %fusion.182) | copy-start | bytes 3076
  119.7 34.5 %copy-start.70 = (f32[256]{0:T(256)}, f32[256]{0:T(256)S(1)}, u32[]{:S(2)}) copy-start(f32[256]{0:T(256)S(1)} %select_reduce_fusion.3) | copy-start | bytes 3076
  132.3 21.8 %collective-permute-start.5 = (bf16[256,768]{1,0:T(8,128)(2,1)}, bf16[256,768]{1,0:T(8,128)(2,1)}, u32[]{:S(2)}, u32[]{:S(2)}) collective-permute-start(bf16[256,768]{1,0:T(8,128)(2,1)} %slice_bitcast_fusion.17), channel_id=1, source_target_pairs={{0,1},{1,0},{2,3},{3,2},{4,5},{5,4},{6,7},{7,6},{8,9},{9,8},{10,11... | collective-permute-start | bytes 1179656 | tf_op jit(solution)/shard_map/ppermute | solution.py:16
  160.7 3.9 collective-permute-start.6
  167.9 31.6 %copy-start.65 = (f32[256]{0:T(256)}, f32[256]{0:T(256)S(1)}, u32[]{:S(2)}) copy-start(f32[256]{0:T(256)S(1)} %select_reduce_fusion.2) | copy-start | bytes 3076
  168.9 31.8 %copy-start.91 = (bf16[1,1,768,1536]{3,2,1,0:T(8,128)(2,1)S(1)}, bf16[1,1,768,1536]{3,2,1,0:T(8,128)(2,1)}, u32[]{:S(2)}) copy-start(bf16[1,1,768,1536]{3,2,1,0:T(8,128)(2,1)} %param.22) | copy-start | bytes 7077892
  234.9 27.5 %all-to-all-start.4 = ((bf16[64,16,768]{2,1,0:T(8,128)(2,1)}), bf16[64,16,768]{2,1,0:T(8,128)(2,1)}, u32[]{:S(2)}, u32[]{:S(2)}) async-start(bf16[64,16,768]{2,1,0:T(8,128)(2,1)} %pad_maximum_fusion.2), calls=%async_computation.4 | async-start | bytes 3145728 | tf_op jit(solution)/shard_map/all_to_all | solution.py:224
  242.5 27.0 %copy-start.83 = (pred[256]{0:T(512)(128)(4,1)S(1)}, pred[256]{0:T(512)(128)(4,1)}, u32[]{:S(2)}) copy-start(pred[256]{0:T(512)(128)(4,1)} %get-tuple-element.24) | copy-start | bytes 772
  263.6 5.9 %collective-permute-start.7 = (bf16[256,768]{1,0:T(8,128)(2,1)S(1)}, bf16[256,768]{1,0:T(8,128)(2,1)S(1)}, u32[]{:S(2)}, u32[]{:S(2)}) collective-permute-start(bf16[256,768]{1,0:T(8,128)(2,1)S(1)} %get-tuple-element.43), channel_id=1, source_target_pairs={{0,1},{1,0},{2,3},{3,2},{4,5},{5,4},{6,7},{7,6},{8,9},{9,8},{10,11... | collective-permute-start | bytes 1179656 | tf_op jit(solution)/shard_map/ppermute | solution.py:16
  266.6 4.1 collective-permute-start.9
  285.5 3.6 collective-permute-start.10
  295.6 27.9 %all-to-all-start.5 = ((bf16[64,8,768]{2,1,0:T(8,128)(2,1)}), bf16[64,8,768]{2,1,0:T(8,128)(2,1)}, u32[]{:S(2)}, u32[]{:S(2)}) async-start(bf16[64,8,768]{2,1,0:T(8,128)(2,1)} %pad_maximum_fusion.14), calls=%async_computation.5 | async-start | bytes 1572864 | tf_op jit(solution)/shard_map/all_to_all | solution.py:220
  305.2 16.3 %collective-permute-start.8 = (f32[256,384]{1,0:T(8,128)}, f32[256,384]{1,0:T(8,128)}, u32[]{:S(2)}, u32[]{:S(2)}) collective-permute-start(f32[256,384]{1,0:T(8,128)} %get-tuple-element.22), channel_id=1, source_target_pairs={{0,64},{64,0},{1,65},{65,1},{2,66},{66,2},{3,67},{67,3},{4,68},{68... | collective-permute-start | bytes 1179656 | tf_op jit(solution)/shard_map/ppermute | solution.py:16
  331.7 18.7 %copy-start.41 = (f32[256,384]{1,0:T(8,128)S(1)}, f32[256,384]{1,0:T(8,128)}, u32[]{:S(2)}) copy-start(f32[256,384]{1,0:T(8,128)} %get-tuple-element.44) | copy-start | bytes 1179652
  340.2 12.2 %copy-start.86 = (f32[256]{0:T(256)S(1)}, f32[256]{0:T(256)}, u32[]{:S(2)}) copy-start(f32[256]{0:T(256)} %get-tuple-element.20) | copy-start | bytes 3076
  340.2 12.2 %copy-start.82 = (bf16[768]{0:T(1024)(128)(2,1)S(1)}, bf16[768]{0:T(1024)(128)(2,1)}, u32[]{:S(2)}) copy-start(bf16[768]{0:T(1024)(128)(2,1)} %get-tuple-element.9) | copy-start | bytes 4612
  340.2 12.4 %copy-start.16 = (bf16[256,768]{1,0:T(8,128)(2,1)S(1)}, bf16[256,768]{1,0:T(8,128)(2,1)}, u32[]{:S(2)}) copy-start(bf16[256,768]{1,0:T(8,128)(2,1)} %copy-done.15) | copy-start | bytes 1179652
  340.2 12.5 %copy-start.58 = (s32[256]{0:T(256)S(1)}, s32[256]{0:T(256)}, u32[]{:S(2)}) copy-start(s32[256]{0:T(256)} %copy-done.57) | copy-start | bytes 3076
  340.2 12.5 %copy-start.62 = (f32[256]{0:T(256)S(1)}, f32[256]{0:T(256)}, u32[]{:S(2)}) copy-start(f32[256]{0:T(256)} %copy-done.61) | copy-start | bytes 3076
  340.2 22.8 %all-to-all-start.6 = ((bf16[64,8,768]{2,1,0:T(8,128)(2,1)}), bf16[64,8,768]{2,1,0:T(8,128)(2,1)}, u32[]{:S(2)}, u32[]{:S(2)}) async-start(bf16[64,8,768]{2,1,0:T(8,128)(2,1)} %fusion.58), calls=%async_computation.6 | async-start | bytes 1572864 | tf_op jit(solution)/shard_map/all_to_all | solution.py:224
  357.0 16.2 %copy-start.14 = (bf16[64,16,768]{2,1,0:T(8,128)(2,1)S(1)}, bf16[64,16,768]{2,1,0:T(8,128)(2,1)}, u32[]{:S(2)}) copy-start(bf16[64,16,768]{2,1,0:T(8,128)(2,1)} %copy-done.13) | copy-start | bytes 4718596
  363.0 51.4 %all-to-all-start.8 = ((bf16[32,104,384]{2,1,0:T(8,128)(2,1)}), bf16[32,104,384]{2,1,0:T(8,128)(2,1)}, u32[]{:S(2)}, u32[]{:S(2)}) async-start(bf16[32,104,384]{2,1,0:T(8,128)(2,1)} %pad_maximum_fusion.1), calls=%async_computation.8 | async-start | bytes 5111808 | tf_op jit(solution)/shard_map/all_to_all | solution.py:402
  370.4 7.6 %collective-permute-start.11 = (bf16[256,768]{1,0:T(8,128)(2,1)S(1)}, bf16[256,768]{1,0:T(8,128)(2,1)S(1)}, u32[]{:S(2)}, u32[]{:S(2)}) collective-permute-start(bf16[256,768]{1,0:T(8,128)(2,1)S(1)} %slice_bitcast_fusion.14), channel_id=1, source_target_pairs={{0,1},{1,0},{2,3},{3,2},{4,5},{5,4},{6,7},{7,6},{8,9},{9,8},{10,11... | collective-permute-start | bytes 1179656 | tf_op jit(solution)/shard_map/ppermute | solution.py:16
  375.9 15.5 %collective-permute-start.15 = (bf16[512,768]{1,0:T(8,128)(2,1)}, bf16[512,768]{1,0:T(8,128)(2,1)}, u32[]{:S(2)}, u32[]{:S(2)}) collective-permute-start(bf16[512,768]{1,0:T(8,128)(2,1)} %get-tuple-element.39), channel_id=1, source_target_pairs={{0,1},{1,0},{2,3},{3,2},{4,5},{5,4},{6,7},{7,6},{8,9},{9,8},{10,11... | collective-permute-start | bytes 2359304 | tf_op jit(solution)/shard_map/ppermute | solution.py:16
  376.0 48.3 %collective-permute-start.16 = (bf16[512,768]{1,0:T(8,128)(2,1)}, bf16[512,768]{1,0:T(8,128)(2,1)}, u32[]{:S(2)}, u32[]{:S(2)}) collective-permute-start(bf16[512,768]{1,0:T(8,128)(2,1)} %get-tuple-element.38), channel_id=1, source_target_pairs={{0,1},{1,0},{2,3},{3,2},{4,5},{5,4},{6,7},{7,6},{8,9},{9,8},{10,11... | collective-permute-start | bytes 2359304 | tf_op jit(solution)/shard_map/ppermute | solution.py:16
  391.2 17.4 %collective-permute-start.12 = (f32[256,768]{1,0:T(8,128)S(1)}, f32[256,768]{1,0:T(8,128)}, u32[]{:S(2)}, u32[]{:S(2)}) collective-permute-start(f32[256,768]{1,0:T(8,128)S(1)} %convolution_bitcast_fusion.2), channel_id=1, source_target_pairs={{0,1},{1,0},{2,3},{3,2},{4,5},{5,4},{6,7},{7,6},{8,9},{9,8},{10,11... | collective-permute-start | bytes 2359304 | tf_op jit(solution)/shard_map/ppermute | solution.py:16
  414.4 44.6 %all-to-all-start.7 = ((bf16[32,104,384]{2,1,0:T(8,128)(2,1)}), bf16[32,104,384]{2,1,0:T(8,128)(2,1)}, u32[]{:S(2)}, u32[]{:S(2)}) async-start(bf16[32,104,384]{2,1,0:T(8,128)(2,1)} %pad_maximum_fusion), calls=%async_computation.7 | async-start | bytes 5111808 | tf_op jit(solution)/shard_map/all_to_all | solution.py:402
  448.7 19.0 %collective-permute-start.13 = (f32[256,384]{1,0:T(8,128)S(1)}, f32[256,384]{1,0:T(8,128)S(1)}, u32[]{:S(2)}, u32[]{:S(2)}) collective-permute-start(f32[256,384]{1,0:T(8,128)S(1)} %get-tuple-element.17), channel_id=1, source_target_pairs={{0,64},{64,0},{1,65},{65,1},{2,66},{66,2},{3,67},{67,3},{4,68},{68... | collective-permute-start | bytes 1179656 | tf_op jit(solution)/shard_map/ppermute | solution.py:16
  461.2 10.0 %collective-permute-start.14 = (f32[104,384]{1,0:T(8,128)S(1)}, f32[104,384]{1,0:T(8,128)S(1)}, u32[]{:S(2)}, u32[]{:S(2)}) collective-permute-start(f32[104,384]{1,0:T(8,128)S(1)} %broadcast_select_fusion.4), channel_id=1, source_target_pairs={{0,64},{64,0},{1,65},{65,1},{2,66},{66,2},{3,67},{67,3},{4,68},{68... | collective-permute-start | bytes 479240 | tf_op jit(solution)/shard_map/ppermute | solution.py:16
  (75 other events, 282.2 us)
Sparse Core Ops, SparseCore 0:
  73.8 73.4 all-gather.2
